TPU v7x, 32 devices: a whole 2x2x4 slice. The times are simulated.
32 devices in a mesh: section: 2 (over core), expert: 4 (over z), mp: 4 (over y, x).
Axes of the slice: x: 2, y: 2, z: 4, core: 2. Of those that a mesh axis runs over, the one named last changes fastest.
Arguments:
- layer_inputs: bfloat16 [2, 1024, 2048], P('section', ('expert', 'mp')), may hold values from -6 to 6
- norm_gain: float32 [2, 2048], P('section'), may hold values from 0.1 to 1.9
- w_gate: bfloat16 [2, 64, 768, 2048], P('section', 'expert', 'mp'), may hold values from -0.125 to 0.125
- w_up: bfloat16 [2, 64, 768, 2048], P('section', 'expert', 'mp'), may hold values from -0.125 to 0.125
- w_down: bfloat16 [2, 64, 768, 2048], P('section', 'expert', 'mp'), may hold values from -0.21875 to 0.21875
- routes: int32 [2, 1024, 8], P('section', ('expert', 'mp')), may hold values from 0 to 63, all different within a row; in each aligned block of 32 rows (0 to 31, 32 to 63, ..., all dimensions but the last counted through in order) at most 5 rows name the same one
- probs: float32 [2, 1024, 8], P('section', ('expert', 'mp')), may hold values from 0.05 to 0.3
- cotangent: bfloat16 [1024, 2048], P(('expert', 'mp')), may hold values from -6 to 6
- sampled: int32 [1], replicated, may hold values from 0 to 1
Outputs:
- input_grads: bfloat16 [2, 1024, 2048], P('section', ('expert', 'mp'))
- gate_grads: float32 [2, 64, 768, 2048], P('section', 'expert', 'mp')
- up_grads: float32 [2, 64, 768, 2048], P('section', 'expert', 'mp')
Inputs may be any that keep to these rules, and one draw needn't show every extreme that they name: `routes`: each row names 8 different experts and every expert is named somewhere. In each aligned block of 32 rows of a layer, no expert is named by more than 5 rows, and in some blocks one expert is named by exactly 5.
All inputs are finite; a program needn't handle non-finite values.
Results may differ from a plain program's by a relative error of at most 0.012.
Values may be sent and summed in bfloat16 or wider, within the bound.
A program may use at most 384 MiB of HBM per device.

v0:
```python
import jax
import jax.numpy as jnp
from jax import lax
from jax.sharding import PartitionSpec as P

CAPH = 5


epsilon = 1e-06


def shifted(x, axis, by):
    peers = lax.axis_size(axis)
    pairs = [(i, i + by) for i in range(peers) if 0 <= i + by < peers]
    return lax.ppermute(x, axis, pairs)


def normalize(inputs, gain_vector):
    values = inputs.astype(jnp.float32)
    factor = lax.rsqrt(jnp.mean(values * values, axis=1, keepdims=True) + epsilon)
    normed = values * factor
    return (normed, factor, (normed * gain_vector[None, :]).astype(jnp.bfloat16))


def slot_targets(block_routes, experts, capacity):
    flat_routes = block_routes.reshape(-1)
    onehot = (flat_routes[:, None] == jnp.arange(experts, dtype=jnp.int32)[None, :]).astype(
        jnp.int32
    )
    earlier = jnp.cumsum(onehot, axis=0) - onehot
    places = jnp.sum(earlier * onehot, axis=1)
    return flat_routes * capacity + places


def expert_pass(hidden_rows, weighted_rows, gate_w, up_w, down_w):
    gate_act = jnp.einsum("slcd,lfd->slcf", hidden_rows, gate_w, preferred_element_type=jnp.float32)
    lifted = jnp.einsum("slcd,lfd->slcf", hidden_rows, up_w, preferred_element_type=jnp.float32)
    back = jnp.einsum("slcd,lfd->slcf", weighted_rows, down_w, preferred_element_type=jnp.float32)
    logistic = jax.nn.sigmoid(gate_act)
    d_gate = (back * lifted * logistic * (1.0 + gate_act * (1.0 - logistic))).astype(jnp.bfloat16)
    d_up = (back * gate_act * logistic).astype(jnp.bfloat16)
    partial_rows = jnp.einsum("slcf,lfd->slcd", d_gate, gate_w, preferred_element_type=jnp.float32)
    partial_rows = partial_rows + jnp.einsum(
        "slcf,lfd->slcd", d_up, up_w, preferred_element_type=jnp.float32
    )
    return (partial_rows, d_gate, d_up)


def per_device(layer_inputs, norm_gain, w_gate, w_up, w_down, routes, probs, cotangent, sampled):
    section_index = lax.axis_index("section")
    n_expert = lax.axis_size("expert")
    gate_w, up_w, down_w = (
        lax.all_gather(w_gate[0], "mp", axis=1, tiled=True),
        lax.all_gather(w_up[0], "mp", axis=1, tiled=True),
        lax.all_gather(w_down[0], "mp", axis=1, tiled=True),
    )
    tok_rows = cotangent.shape[0]
    feature_width = cotangent.shape[1]
    local_experts = gate_w.shape[0]
    hidden_units = gate_w.shape[1]
    experts = local_experts * n_expert
    top_count = routes.shape[2]
    block_count = 2
    block_rows = tok_rows // block_count
    capacity = CAPH * 2 // block_count
    gain_vector = norm_gain[0]
    normed, factor, hidden = normalize(layer_inputs[0], gain_vector)
    training = sampled[0] == section_index
    result = jnp.zeros((tok_rows, feature_width), jnp.bfloat16)
    received = jnp.zeros((block_rows, feature_width), jnp.bfloat16)
    hidden_list = []
    gate_list = []
    up_list = []
    for step_index in range(block_count + 1):
        micro_index = step_index - 1 + section_index
        is_valid = jnp.logical_and(micro_index >= 0, micro_index < block_count)
        row_start = jnp.clip(micro_index, 0, block_count - 1) * block_rows
        if step_index < block_count:
            own_rows = cotangent[step_index * block_rows : (step_index + 1) * block_rows]
        else:
            own_rows = jnp.zeros((block_rows, feature_width), jnp.bfloat16)
        upstream = jnp.where(section_index == 1, own_rows, received)
        upstream = jnp.where(is_valid, upstream, jnp.zeros_like(upstream))
        block_hidden = lax.dynamic_slice_in_dim(hidden, row_start, block_rows, 0)
        block_normed = lax.dynamic_slice_in_dim(normed, row_start, block_rows, 0)
        block_factor = lax.dynamic_slice_in_dim(factor, row_start, block_rows, 0)
        block_routes = lax.dynamic_slice_in_dim(routes[0], row_start, block_rows, 0)
        block_probs = lax.dynamic_slice_in_dim(probs[0], row_start, block_rows, 0)
        targets = slot_targets(block_routes, experts, capacity)
        hidden_slots = jnp.repeat(block_hidden, top_count, axis=0)
        weighted_slots = (
            block_probs[:, :, None] * upstream[:, None, :].astype(jnp.float32)
        ).astype(jnp.bfloat16)
        weighted_slots = weighted_slots.reshape(block_rows * top_count, feature_width)
        hidden_buffer = (
            jnp.zeros((experts * capacity, feature_width), jnp.bfloat16)
            .at[targets]
            .set(hidden_slots)
        )
        hidden_buffer = hidden_buffer.reshape(n_expert, local_experts * capacity, feature_width)
        weighted_buffer = (
            jnp.zeros((experts * capacity, feature_width), jnp.bfloat16)
            .at[targets]
            .set(weighted_slots)
        )
        weighted_buffer = weighted_buffer.reshape(n_expert, local_experts * capacity, feature_width)
        hidden_rows, weighted_rows = (
            lax.all_to_all(hidden_buffer, "expert", split_axis=0, concat_axis=0, tiled=True),
            lax.all_to_all(weighted_buffer, "expert", split_axis=0, concat_axis=0, tiled=True),
        )
        hidden_rows = hidden_rows.reshape(n_expert, local_experts, capacity, feature_width)
        weighted_rows = weighted_rows.reshape(n_expert, local_experts, capacity, feature_width)

        def compute_block(operands):
            return expert_pass(operands[0], operands[1], gate_w, up_w, down_w)

        def skip_block(operands):
            row_shape = operands[0].shape[:3]
            return (
                jnp.zeros(row_shape + (feature_width,), jnp.float32),
                jnp.zeros(row_shape + (hidden_units,), jnp.bfloat16),
                jnp.zeros(row_shape + (hidden_units,), jnp.bfloat16),
            )

        partial_rows, d_gate, d_up = lax.cond(
            is_valid, compute_block, skip_block, (hidden_rows, weighted_rows)
        )
        slot_grad = partial_rows.astype(jnp.bfloat16).reshape(
            n_expert, local_experts * capacity, feature_width
        )
        returned = lax.all_to_all(slot_grad, "expert", split_axis=0, concat_axis=0, tiled=True)
        slot_values = returned.reshape(experts * capacity, feature_width)[targets]
        token_grad = jnp.sum(
            slot_values.reshape(block_rows, top_count, feature_width).astype(jnp.float32), axis=1
        )
        scaled = token_grad * gain_vector[None, :]
        inner = jnp.mean(scaled * block_normed, axis=1, keepdims=True)
        input_grad = (
            upstream.astype(jnp.float32) + block_factor * (scaled - block_normed * inner)
        ).astype(jnp.bfloat16)
        current = lax.dynamic_slice_in_dim(result, row_start, block_rows, 0)
        result = lax.dynamic_update_slice_in_dim(
            result, jnp.where(is_valid, input_grad, current), row_start, 0
        )
        hidden_list.append(hidden_rows)
        gate_list.append(d_gate)
        up_list.append(d_up)
        if step_index < block_count:
            received = shifted(input_grad, "section", -1)
    upper_section = section_index == 1

    def pick_valid(stored):
        stacked = jnp.stack(stored)
        return jnp.where(upper_section, stacked[:block_count], stacked[1:])

    hidden_store = pick_valid(hidden_list)
    gate_store = pick_valid(gate_list)
    up_store = pick_valid(up_list)
    all_hidden = lax.all_gather(hidden_store[None], "mp", axis=0, tiled=True)
    gate_parts, up_parts = (
        lax.all_to_all(gate_store[None], "mp", split_axis=5, concat_axis=0, tiled=True),
        lax.all_to_all(up_store[None], "mp", split_axis=5, concat_axis=0, tiled=True),
    )

    def weigh_rows(operands):
        gate_in, up_in, rows_in = operands
        gate_terms = jnp.einsum(
            "mbslcf,mbslcd->mlfd", gate_in, rows_in, preferred_element_type=jnp.float32
        )
        up_terms = jnp.einsum(
            "mbslcf,mbslcd->mlfd", up_in, rows_in, preferred_element_type=jnp.float32
        )
        gate_terms = lax.optimization_barrier(gate_terms.astype(jnp.bfloat16)).astype(jnp.float32)
        up_terms = lax.optimization_barrier(up_terms.astype(jnp.bfloat16)).astype(jnp.float32)
        return (jnp.sum(gate_terms, axis=0), jnp.sum(up_terms, axis=0))

    def zero_rows(operands):
        share_shape = (local_experts, operands[0].shape[-1], feature_width)
        return (jnp.zeros(share_shape, jnp.float32), jnp.zeros(share_shape, jnp.float32))

    gate_share, up_share = lax.cond(
        training, weigh_rows, zero_rows, (gate_parts, up_parts, all_hidden)
    )
    return (result[None], gate_share[None], up_share[None])


def solution(mesh):
    placed = (
        P("section", ("expert", "mp"), None),
        P("section", None),
        P("section", "expert", "mp", None),
        P("section", "expert", "mp", None),
        P("section", "expert", "mp", None),
        P("section", ("expert", "mp"), None),
        P("section", ("expert", "mp"), None),
        P(("expert", "mp"), None),
        P(),
    )
    return jax.shard_map(
        per_device,
        mesh=mesh,
        in_specs=placed,
        out_specs=(
            P("section", ("expert", "mp"), None),
            P("section", "expert", "mp", None),
            P("section", "expert", "mp", None),
        ),
        check_vma=False,
    )
```

profile of v0, /device:TPU:0, one launch (start us, length us, event | category | flops | bytes accessed | tf_op | source)
XLA Modules:
  0.0 2145.8 jit_solution(14293377435592193434)
XLA Ops:
  26.2 27.1 %all-to-all-done.1 = bf16[4,80,2048]{2,1,0:T(8,128)(2,1)S(1)} async-done(((bf16[4,80,2048]{2,1,0:T(8,128)(2,1)}), bf16[4,80,2048]{2,1,0:T(8,128)(2,1)S(1)}, u32[]{:S(2)}, u32[]{:S(2)}) %all-to-all-start.1) | async-done | bytes 1310752 | tf_op jit(solution)/shard_map/all_to_all | solution.py:108
  63.4 24.2 %all-to-all-done = bf16[4,80,2048]{2,1,0:T(8,128)(2,1)S(1)} async-done(((bf16[4,80,2048]{2,1,0:T(8,128)(2,1)}), bf16[4,80,2048]{2,1,0:T(8,128)(2,1)S(1)}, u32[]{:S(2)}, u32[]{:S(2)}) %all-to-all-start) | async-done | bytes 1310752 | tf_op jit(solution)/shard_map/all_to_all | solution.py:109
  95.9 26.1 %all-to-all-done.4 = bf16[4,80,2048]{2,1,0:T(8,128)(2,1)S(1)} async-done(((bf16[4,80,2048]{2,1,0:T(8,128)(2,1)}), bf16[4,80,2048]{2,1,0:T(8,128)(2,1)S(1)}, u32[]{:S(2)}, u32[]{:S(2)}) %all-to-all-start.4) | async-done | bytes 1310752 | tf_op jit(solution)/shard_map/all_to_all | solution.py:108
  125.6 324.9 %all-gather.10.cloned.1.call-done = bf16[1,16,768,2048]{3,2,1,0:T(8,128)(2,1)} async-done(((bf16[1,16,192,2048]{3,2,1,0:T(8,128)(2,1)}), bf16[1,16,768,2048]{3,2,1,0:T(8,128)(2,1)}) %all-gather.10.cloned.1.call-update) | async-done | bytes 50331664 | tf_op jit(solution)/shard_map/all_gather | solution.py:55
  450.5 439.8 %all-gather.12.cloned.1.call-done = bf16[1,16,768,2048]{3,2,1,0:T(8,128)(2,1)} async-done(((bf16[1,16,192,2048]{3,2,1,0:T(8,128)(2,1)}), bf16[1,16,768,2048]{3,2,1,0:T(8,128)(2,1)}) %all-gather.12.cloned.1.call-update) | async-done | bytes 50331664 | tf_op jit(solution)/shard_map/all_gather | solution.py:54
  890.3 439.8 %all-gather.14.cloned.1.call-done = bf16[1,16,768,2048]{3,2,1,0:T(8,128)(2,1)} async-done(((bf16[1,16,192,2048]{3,2,1,0:T(8,128)(2,1)}), bf16[1,16,768,2048]{3,2,1,0:T(8,128)(2,1)}) %all-gather.14.cloned.1.call-update) | async-done | bytes 50331664 | tf_op jit(solution)/shard_map/all_gather | solution.py:53
  1330.0 10.9 conditional.4
  1375.2 105.6 %collective-permute-done = bf16[32,2048]{1,0:T(8,128)(2,1)S(1)} collective-permute-done((bf16[32,2048]{1,0:T(8,128)(2,1)S(1)}, bf16[32,2048]{1,0:T(8,128)(2,1)S(1)}, u32[]{:S(2)}, u32[]{:S(2)}) %collective-permute-start) | collective-permute-done | bytes 131104 | tf_op jit(solution)/shard_map/ppermute | solution.py:15
  1489.4 32.0 %all-to-all-done.3 = bf16[4,80,2048]{2,1,0:T(8,128)(2,1)} async-done(((bf16[4,80,2048]{2,1,0:T(8,128)(2,1)}), bf16[4,80,2048]{2,1,0:T(8,128)(2,1)}, u32[]{:S(2)}, u32[]{:S(2)}) %all-to-all-start.3) | async-done | bytes 1310752 | tf_op jit(solution)/shard_map/all_to_all | solution.py:109
  1521.4 116.9 %conditional.5 = (bf16[4,16,5,2048]{3,2,0,1:T(8,128)(2,1)}, bf16[1,1,4,16,5,768]{5,3,4,2,1,0:T(8,128)(2,1)}, bf16[1,1,4,16,5,768]{5,3,4,2,1,0:T(8,128)(2,1)}) conditional(s32[]{:T(128)} %convert_element_type.148, () %tuple.70, (bf16[4,80,2048]{2,1,0:T(8,128)(2,1)}, bf16[16,768,2048]{2,1,0:T(8,128)(2,1)}, bf16[4,80,2048]{2,1,0:T(8,128)(2,1)S(1)}, ...), branch_computations={%region_15.16_spmd, %region_16.17_spmd} | conditional | flops 5038407680 | bytes 278200384 | solution.py:125
  1524.7 21.6 %fusion.32 = f32[16,768,4,5]{1,3,2,0:T(8,128)} fusion(bf16[16,768,2048]{2,1,0:T(8,128)(2,1)} %get-tuple-element.63, bf16[4,16,5,2048]{3,0,2,1:T(4,128)(2,1)} %bitcast.391), kind=kOutput, calls=%fused_computation.40 | convolution fusion | flops 1006632960 | bytes 52625408 | tf_op jit(solution)/shard_map/cond/branch_1_fun/slcd,lfd->slcf/dot_general | solution.py:38
  1548.4 22.5 %fusion.50 = (bf16[4,16,5,768]{3,2,0,1:T(8,128)(2,1)S(1)}, f32[16,768,4,5]{1,3,2,0:T(8,128)}) fusion(f32[16,768,4,5]{1,3,2,0:T(8,128)} %fusion.32, bf16[4,16,5,2048]{3,0,2,1:T(4,128)(2,1)} %bitcast.386, bf16[16,768,2048]{2,1,0:T(8,128)(2,1)} %get-tuple-element.67), kind=kOutput, calls=%fused_computation.60 | convolution fusion | flops 1008107520 | bytes 54099968 | tf_op jit(solution)/shard_map/cond/branch_1_fun/slcd,lfd->slcf/dot_general | solution.py:36
  1571.0 22.9 %fusion.48 = bf16[4,16,5,768]{3,2,0,1:T(8,128)(2,1)} fusion(f32[16,768,4,5]{1,3,2,0:T(8,128)} %get-tuple-element.177, f32[16,768,4,5]{1,3,2,0:T(8,128)} %fusion.32, bf16[4,16,5,2048]{3,0,2,1:T(4,128)(2,1)} %bitcast.387, bf16[16,768,2048]{2,1,0:T(8,128)(2,1)} %get-tuple-element.65), kind=kOutput, calls=%fused_computation.58 | convolution fusion | flops 1009090560 | bytes 54099968 | tf_op jit(solution)/shard_map/cond/branch_1_fun/slcd,lfd->slcf/dot_general | solution.py:37
  1593.9 21.4 fusion.28
  1615.2 20.8 add_bitcast_fusion.1
  1646.5 31.1 %all-to-all-done.5 = bf16[4,80,2048]{2,1,0:T(8,128)(2,1)S(1)} async-done(((bf16[4,80,2048]{2,1,0:T(8,128)(2,1)}), bf16[4,80,2048]{2,1,0:T(8,128)(2,1)S(1)}, u32[]{:S(2)}, u32[]{:S(2)}) %all-to-all-start.5) | async-done | bytes 1310752 | tf_op jit(solution)/shard_map/all_to_all | solution.py:131
  1692.8 31.9 %all-to-all-done.6 = bf16[4,80,2048]{2,1,0:T(8,128)(2,1)S(1)} async-done(((bf16[4,80,2048]{2,1,0:T(8,128)(2,1)}), bf16[4,80,2048]{2,1,0:T(8,128)(2,1)S(1)}, u32[]{:S(2)}, u32[]{:S(2)}) %all-to-all-start.6) | async-done | bytes 1310752 | tf_op jit(solution)/shard_map/all_to_all | solution.py:109
  1724.7 113.1 %conditional.6 = (bf16[4,16,5,2048]{3,2,0,1:T(8,128)(2,1)}, bf16[1,1,4,16,5,768]{5,3,4,2,1,0:T(8,128)(2,1)S(1)}, bf16[1,1,4,16,5,768]{5,3,4,2,1,0:T(8,128)(2,1)}) conditional(s32[]{:T(128)} %convert_element_type.157, () %tuple.72, (bf16[4,80,2048]{2,1,0:T(8,128)(2,1)S(1)}, bf16[16,768,2048]{2,1,0:T(8,128)(2,1)}, ...), branch_computations={%region_24.25_spmd, %region_25.26_spmd} | conditional | flops 5038407680 | bytes 281477184 | solution.py:125
  1726.7 21.8 %fusion.60 = f32[16,768,4,5]{1,3,2,0:T(8,128)} fusion(bf16[16,768,2048]{2,1,0:T(8,128)(2,1)} %get-tuple-element.68, bf16[4,16,5,2048]{3,0,2,1:T(4,128)(2,1)} %bitcast.392), kind=kOutput, calls=%fused_computation.67 | convolution fusion | flops 1006632960 | bytes 52625408 | tf_op jit(solution)/shard_map/cond/branch_1_fun/slcd,lfd->slcf/dot_general | solution.py:38
  1750.6 22.6 %fusion.78 = (bf16[4,16,5,768]{3,2,0,1:T(8,128)(2,1)S(1)}, f32[16,768,4,5]{1,3,2,0:T(8,128)}) fusion(f32[16,768,4,5]{1,3,2,0:T(8,128)} %fusion.60, bf16[4,16,5,2048]{3,0,2,1:T(4,128)(2,1)} %bitcast.388, bf16[16,768,2048]{2,1,0:T(8,128)(2,1)} %get-tuple-element.72), kind=kOutput, calls=%fused_computation.87 | convolution fusion | flops 1008107520 | bytes 54099968 | tf_op jit(solution)/shard_map/cond/branch_1_fun/slcd,lfd->slcf/dot_general | solution.py:36
  1773.2 21.9 %fusion.76 = bf16[4,16,5,768]{3,2,0,1:T(8,128)(2,1)S(1)} fusion(f32[16,768,4,5]{1,3,2,0:T(8,128)} %get-tuple-element.179, f32[16,768,4,5]{1,3,2,0:T(8,128)} %fusion.60, bf16[4,16,5,2048]{3,0,2,1:T(4,128)(2,1)S(1)} %bitcast.389, bf16[16,768,2048]{2,1,0:T(8,128)(2,1)} %get-tuple-element.70), kind=kOutput, calls=%fused_computation.85 | convolution fusion | flops 1009090560 | bytes 54099968 | tf_op jit(solution)/shard_map/cond/branch_1_fun/slcd,lfd->slcf/dot_general | solution.py:37
  1795.2 19.9 fusion.56
  1815.1 20.9 add_bitcast_fusion.2
  1870.2 16.5 broadcast_select_fusion
  1900.5 10.3 reshape.546
  1937.0 15.0 copy.221
  1958.7 15.0 copy.222
  1973.7 159.3 %conditional.7 = (f32[1,16,192,2048]{3,2,1,0:T(8,128)}, f32[1,16,192,2048]{3,2,1,0:T(8,128)}) conditional(s32[]{:T(128)} %convert_element_type.165, () %tuple.74, (bf16[4,1,2,4,16,5,192]{6,0,4,5,3,2,1:T(4,128)(2,1)S(1)}, bf16[4,2,4,16,5,2048]{5,3,4,2,1,0:T(8,128)(2,1)}, bf16[4,1,2,4,16,5,192]{6,0,4,5,3,2,1:T(4,128)(2,1)S(1)}) %tuple.150), branch_computations={%region_28.29_spmd, %region_29.32_spmd} | conditional | flops 4164943872 | bytes 316538944 | solution.py:181
  1984.1 34.7 %bitcast_convert_fusion.1 = bf16[4,16,192,2048]{3,2,1,0:T(8,128)(2,1)} fusion(bf16[4,2,4,16,5,2048]{5,3,4,2,1,0:T(8,128)(2,1)} %get-tuple-element.156, bf16[4,1,2,4,16,5,192]{6,0,4,5,3,2,1:T(4,128)(2,1)S(1)} %get-tuple-element.155), kind=kOutput, calls=%fused_computation.91 | convolution fusion | flops 2038431744 | bytes 61800448 | tf_op jit(solution)/shard_map/cond/branch_1_fun/mbslcf,mbslcd->mlfd/dot_general | solution.py:167
  2018.8 37.7 %convert_reduce_fusion.1 = f32[16,192,2048]{2,1,0:T(8,128)} fusion(bf16[4,16,192,2048]{3,2,1,0:T(8,128)(2,1)} %bitcast_convert_fusion.1), kind=kLoop, calls=%fused_computation.93 | loop fusion | flops 44040192 | bytes 75497472 | tf_op jit(solution)/shard_map/cond/branch_1_fun/reduce_sum | solution.py:175
  2056.6 39.2 %bitcast_convert_fusion = bf16[4,16,192,2048]{3,2,1,0:T(8,128)(2,1)} fusion(bf16[4,2,4,16,5,2048]{5,3,4,2,1,0:T(8,128)(2,1)S(1)} %copy-done.35, bf16[4,1,2,4,16,5,192]{6,0,4,5,3,2,1:T(4,128)(2,1)S(1)} %get-tuple-element.157), kind=kOutput, calls=%fused_computation.90 | convolution fusion | flops 2038431744 | bytes 61800448 | tf_op jit(solution)/shard_map/cond/branch_1_fun/mbslcf,mbslcd->mlfd/dot_general | solution.py:170
  2095.8 37.1 %convert_reduce_fusion = f32[16,192,2048]{2,1,0:T(8,128)} fusion(bf16[4,16,192,2048]{3,2,1,0:T(8,128)(2,1)} %bitcast_convert_fusion), kind=kLoop, calls=%fused_computation.92 | loop fusion | flops 44040192 | bytes 75497472 | tf_op jit(solution)/shard_map/cond/branch_1_fun/reduce_sum | solution.py:175
  (205 shorter events, 207.6 us)
Async XLA Ops:
  7.2 443.3 %all-gather.10.cloned.1.call-start = ((), (), s32[]{:S(2)}) async-start(), calls=%async_computation.12 | async-start | bytes 62914560 | tf_op jit(solution)/shard_map/all_gather | solution.py:55
  7.9 882.4 %all-gather.12.cloned.1.call-start = ((), (), s32[]{:S(2)}) async-start(), calls=%async_computation.13 | async-start | bytes 62914560 | tf_op jit(solution)/shard_map/all_gather | solution.py:54
  8.7 1321.4 %all-gather.14.cloned.1.call-start = ((), (), s32[]{:S(2)}) async-start(), calls=%async_computation.14 | async-start | bytes 62914560 | tf_op jit(solution)/shard_map/all_gather | solution.py:53
  11.7 11.1 copy-start.32
  11.9 1670.2 %copy-start.5 = (f32[64,2048]{1,0:T(8,128)}, f32[64,2048]{1,0:T(8,128)S(1)}, u32[]{:S(2)}) copy-start(f32[64,2048]{1,0:T(8,128)S(1)} %get-tuple-element.184) | copy-start | bytes 1572868
  15.5 6.5 copy-start.24
  15.5 7.3 copy-start.16
  15.5 37.8 %all-to-all-start.1 = ((bf16[4,80,2048]{2,1,0:T(8,128)(2,1)}), bf16[4,80,2048]{2,1,0:T(8,128)(2,1)S(1)}, u32[]{:S(2)}, u32[]{:S(2)}) async-start(bf16[4,80,2048]{2,1,0:T(8,128)(2,1)} %bitcast.63), calls=%async_computation.1 | async-start | bytes 2621440 | tf_op jit(solution)/shard_map/all_to_all | solution.py:108
  53.3 10.1 copy-start.3
  53.3 34.4 %all-to-all-start = ((bf16[4,80,2048]{2,1,0:T(8,128)(2,1)}), bf16[4,80,2048]{2,1,0:T(8,128)(2,1)S(1)}, u32[]{:S(2)}, u32[]{:S(2)}) async-start(bf16[4,80,2048]{2,1,0:T(8,128)(2,1)} %bitcast.366), calls=%async_computation | async-start | bytes 2621440 | tf_op jit(solution)/shard_map/all_to_all | solution.py:109
  63.4 27.8 %copy-start.27 = (s32[1,32,8]{1,2,0:T(8,128)S(1)}, s32[1,32,8]{1,2,0:T(8,128)}, u32[]{:S(2)}) copy-start(s32[1,32,8]{1,2,0:T(8,128)} %get-tuple-element.165) | copy-start | bytes 3076
  87.7 8.3 copy-start.7
  87.7 34.3 %all-to-all-start.4 = ((bf16[4,80,2048]{2,1,0:T(8,128)(2,1)}), bf16[4,80,2048]{2,1,0:T(8,128)(2,1)S(1)}, u32[]{:S(2)}, u32[]{:S(2)}) async-start(bf16[4,80,2048]{2,1,0:T(8,128)(2,1)} %bitcast.365), calls=%async_computation.4 | async-start | bytes 2621440 | tf_op jit(solution)/shard_map/all_to_all | solution.py:108
  92.6 29.4 %copy-start.30 = (s32[256,1]{0,1:T(1,128)}, s32[256,1]{0,1:T(1,128)S(1)}, u32[]{:S(2)}) copy-start(s32[256,1]{0,1:T(1,128)S(1)} %compare_select_fusion) | copy-start | bytes 3076
  122.0 1208.0 %copy-start = (bf16[4,80,2048]{2,1,0:T(8,128)(2,1)}, bf16[4,80,2048]{2,1,0:T(8,128)(2,1)S(1)}, u32[]{:S(2)}) copy-start(bf16[4,80,2048]{2,1,0:T(8,128)(2,1)S(1)} %all-to-all-done.4) | copy-start | bytes 3932164
  122.0 1223.6 %all-to-all-start.7 = ((bf16[4,80,2048]{2,1,0:T(8,128)(2,1)}), bf16[4,80,2048]{2,1,0:T(8,128)(2,1)S(1)}, u32[]{:S(2)}, u32[]{:S(2)}) async-start(bf16[4,80,2048]{2,1,0:T(8,128)(2,1)} %bitcast.364), calls=%async_computation.7 | async-start | bytes 2621440 | tf_op jit(solution)/shard_map/all_to_all | solution.py:108
  1345.6 23.3 %all-to-all-start.2 = ((bf16[4,80,2048]{2,1,0:T(8,128)(2,1)}), bf16[4,80,2048]{2,1,0:T(8,128)(2,1)S(1)}, u32[]{:S(2)}, u32[]{:S(2)}) async-start(bf16[4,80,2048]{2,1,0:T(8,128)(2,1)} %copy.170), calls=%async_computation.2 | async-start | bytes 2621440 | tf_op jit(solution)/shard_map/all_to_all | solution.py:131
  1350.2 623.4 %all-gather.8.cloned.1.call-start = ((), (), s32[]{:S(2)}) async-start(), calls=%async_computation.11 | async-start | bytes 13107200 | tf_op jit(solution)/shard_map/all_gather | solution.py:159
  1373.6 107.2 %collective-permute-start = (bf16[32,2048]{1,0:T(8,128)(2,1)S(1)}, bf16[32,2048]{1,0:T(8,128)(2,1)S(1)}, u32[]{:S(2)}, u32[]{:S(2)}) collective-permute-start(bf16[32,2048]{1,0:T(8,128)(2,1)S(1)} %get-tuple-element.171), channel_id=1, source_target_pairs={{16,0},{17,1},{18,2},{19,3},{20,4},{21,5},{22,6},{23,7},{24,8},{25... | collective-permute-start | bytes 393224 | tf_op jit(solution)/shard_map/ppermute | solution.py:15
  1484.9 36.4 %copy-start.2 = (bf16[4,80,2048]{2,1,0:T(8,128)(2,1)S(1)}, bf16[4,80,2048]{2,1,0:T(8,128)(2,1)}, u32[]{:S(2)}) copy-start(bf16[4,80,2048]{2,1,0:T(8,128)(2,1)} %copy-done) | copy-start | bytes 3932164
  1484.9 36.4 %all-to-all-start.3 = ((bf16[4,80,2048]{2,1,0:T(8,128)(2,1)}), bf16[4,80,2048]{2,1,0:T(8,128)(2,1)}, u32[]{:S(2)}, u32[]{:S(2)}) async-start(bf16[4,80,2048]{2,1,0:T(8,128)(2,1)} %bitcast.368), calls=%async_computation.3 | async-start | bytes 2621440 | tf_op jit(solution)/shard_map/all_to_all | solution.py:109
  1615.2 20.8 copy-start.9
  1642.9 34.6 %all-to-all-start.5 = ((bf16[4,80,2048]{2,1,0:T(8,128)(2,1)}), bf16[4,80,2048]{2,1,0:T(8,128)(2,1)S(1)}, u32[]{:S(2)}, u32[]{:S(2)}) async-start(bf16[4,80,2048]{2,1,0:T(8,128)(2,1)} %copy.179), calls=%async_computation.5 | async-start | bytes 2621440 | tf_op jit(solution)/shard_map/all_to_all | solution.py:131
  1679.9 5.6 copy-start.31
  1682.2 247.4 %copy-start.10 = (bf16[64,2048]{1,0:T(8,128)(2,1)}, bf16[64,2048]{1,0:T(8,128)(2,1)S(1)}, u32[]{:S(2)}) copy-start(bf16[64,2048]{1,0:T(8,128)(2,1)S(1)} %get-tuple-element.166) | copy-start | bytes 786436
  1682.2 3.2 collective-permute-start.1
  1689.2 35.4 %all-to-all-start.6 = ((bf16[4,80,2048]{2,1,0:T(8,128)(2,1)}), bf16[4,80,2048]{2,1,0:T(8,128)(2,1)S(1)}, u32[]{:S(2)}, u32[]{:S(2)}) async-start(bf16[4,80,2048]{2,1,0:T(8,128)(2,1)} %bitcast.367), calls=%async_computation.6 | async-start | bytes 2621440 | tf_op jit(solution)/shard_map/all_to_all | solution.py:109
  1750.6 22.6 %copy-start.14 = (bf16[4,80,2048]{2,0,1:T(4,128)(2,1)S(1)}, bf16[4,80,2048]{2,0,1:T(4,128)(2,1)}, u32[]{:S(2)}) copy-start(bf16[4,80,2048]{2,0,1:T(4,128)(2,1)} %copy.186) | copy-start | bytes 3932164 | tf_op jit(solution)/shard_map/cond
  1897.0 13.9 all-to-all-start.9
  1910.8 13.2 all-to-all-start.10
  1924.1 208.9 %all-to-all-start.8 = ((bf16[4,80,2048]{2,1,0:T(8,128)(2,1)}), bf16[4,80,2048]{2,1,0:T(8,128)(2,1)}, u32[]{:S(2)}, u32[]{:S(2)}) async-start(bf16[4,80,2048]{2,1,0:T(8,128)(2,1)} %copy.188), calls=%async_computation.8 | async-start | bytes 2621440 | tf_op jit(solution)/shard_map/all_to_all | solution.py:131
  2018.8 37.7 %copy-start.35 = (bf16[4,2,4,16,5,2048]{5,3,4,2,1,0:T(8,128)(2,1)S(1)}, bf16[4,2,4,16,5,2048]{5,3,4,2,1,0:T(8,128)(2,1)}, u32[]{:S(2)}) copy-start(bf16[4,2,4,16,5,2048]{5,3,4,2,1,0:T(8,128)(2,1)} %get-tuple-element.156) | copy-start | bytes 31457284 | tf_op jit(solution)/shard_map/cond
  (19 other events, 38.4 us)
Sparse Core Ops, SparseCore 0:
  9.9 440.5 all-gather.9
  452.3 437.8 all-gather.11
  892.1 437.8 all-gather.13
  1360.4 211.0 all-gather.7
where the time goes:
time: 2150 us
  waiting for transfers between devices  1500 us (70%)
  matrix products  290 us (13%)
  local copies, waits for them, and re-layouts  158 us (7%)
  other arithmetic  118 us (5%)
  starting transfers between devices  48 us (2%)
    all_gather x1, waiting for transfers between devices, per_device(): lax.all_gather(w_gate[0], 'mp', axis=1, tiled=True)  440 us
    all_gather x1, waiting for transfers between devices, per_device(): lax.all_gather(w_up[0], 'mp', axis=1, tiled=True)  440 us
    all_gather x1, waiting for transfers between devices, per_device(): lax.all_gather(w_down[0], 'mp', axis=1, tiled=True)  325 us
    ppermute x2, waiting for transfers between devices, shifted(): return lax.ppermute(x, axis, pairs)  107 us
    all_to_all x3, waiting for transfers between devices, per_device(): lax.all_to_all(weighted_buffer, 'expert', split_axis=0, concat_axis=0, ti...  88.1 us
    reduce_sum x2, other arithmetic, weigh_rows(): return (jnp.sum(gate_terms, axis=0), jnp.sum(up_terms, axis=0))  74.8 us
    all_to_all x3, waiting for transfers between devices, per_device(): lax.all_to_all(hidden_buffer, 'expert', split_axis=0, concat_axis=0, tile...  53.2 us
    dot_general x2, matrix products, expert_pass(): jnp.einsum('slcd,lfd->slcf', hidden_rows, gate_w, preferred_element_type=...  45.2 us
  transfers between devices with their start and end apart: 17, of which 13 were waited for; matrix products, arithmetic and copies ran while one was open for 26% of the time, Pallas kernels for 0%

commit v1 on v0

v1 whole, which is shorter than its diff:
```python
import jax
import jax.numpy as jnp
from jax import lax
from jax.sharding import PartitionSpec as P

CAPH = 5


epsilon = 1e-06

OWNERS = ("expert", "mp")


def normalize(inputs, gain_vector):
    values = inputs.astype(jnp.float32)
    factor = lax.rsqrt(jnp.mean(values * values, axis=1, keepdims=True) + epsilon)
    normed = values * factor
    return (normed, factor, (normed * gain_vector[None, :]).astype(jnp.bfloat16))


def half_of(x, section_index):
    width = x.shape[-1] // 2
    return lax.dynamic_slice_in_dim(x, section_index * width, width, x.ndim - 1)


def swapped(x):
    return lax.ppermute(x, "section", [(0, 1), (1, 0)])


def joined(mine, other, section_index):
    first = jnp.where(section_index == 0, mine, other)
    second = jnp.where(section_index == 0, other, mine)
    return jnp.concatenate([first, second], axis=-1)


def gather_halves(rows, target, section_index):
    mine = lax.all_gather(half_of(rows, section_index), OWNERS, axis=0, tiled=True)
    other = lax.ppermute(mine, "section", [(1 - target, target)])
    return joined(mine, other, section_index)


def reduce_halves(partial, source, section_index):
    width = partial.shape[-1] // 2
    away, kept = (partial[:, :width], partial[:, width:])
    if source == 0:
        away, kept = (kept, away)
    other = lax.ppermute(away, "section", [(source, 1 - source)])
    mine = jnp.where(section_index == source, kept, other)
    total = lax.psum_scatter(mine, OWNERS, scatter_dimension=0, tiled=True)
    return joined(total, swapped(total), section_index).astype(jnp.float32)


def running_count(present, block_rows):
    counted = present.astype(jnp.bfloat16).reshape(present.shape[0], -1, block_rows)
    inside = jnp.triu(jnp.ones((block_rows, block_rows), jnp.bfloat16))
    within = jnp.einsum("ebi,ij->ebj", counted, inside, preferred_element_type=jnp.float32)
    totals = within[:, :, -1].astype(jnp.bfloat16)
    before = jnp.triu(jnp.ones((totals.shape[1], totals.shape[1]), jnp.bfloat16), 1)
    offset = jnp.einsum("eb,bj->ej", totals, before, preferred_element_type=jnp.float32)
    return (within + offset[:, :, None]).reshape(present.shape).astype(jnp.int32)


def finish(token_grad, gain_vector, normed, factor, upstream):
    scaled = token_grad * gain_vector[None, :]
    inner = jnp.mean(scaled * normed, axis=1, keepdims=True)
    return (upstream.astype(jnp.float32) + factor * (scaled - normed * inner)).astype(jnp.bfloat16)


def per_device(layer_inputs, norm_gain, w_gate, w_up, w_down, routes, probs, cotangent, sampled):
    section_index = lax.axis_index("section")
    gate_w, up_w, down_w = (w_gate[0], w_up[0], w_down[0])
    tok_rows, feature_width = cotangent.shape
    local_experts, units, _ = gate_w.shape
    tokens = tok_rows * lax.axis_size("expert") * lax.axis_size("mp")
    capacity = tokens // (tok_rows // 2) * CAPH
    top_count = routes.shape[2]
    training = sampled[0] == section_index

    gain_vector = norm_gain[0]
    normed, factor, hidden = normalize(layer_inputs[0], gain_vector)
    upper_inputs = swapped(layer_inputs[0])
    upper_gain = swapped(norm_gain[0])

    meta = jnp.concatenate([routes[0].astype(jnp.float32), probs[0]], axis=1)
    meta = lax.all_gather(meta, OWNERS, axis=0, tiled=True)
    all_routes = meta[:, :top_count].astype(jnp.int32)
    all_probs = meta[:, top_count:]
    hidden_all = lax.all_gather(hidden, OWNERS, axis=0, tiled=True)
    cot_all = gather_halves(cotangent, 1, section_index)

    own = lax.axis_index("expert") * local_experts + jnp.arange(local_experts, dtype=jnp.int32)
    match = all_routes[None, :, :] == own[:, None, None]
    present = jnp.any(match, axis=2)
    weight = jnp.sum(jnp.where(match, all_probs[None], 0.0), axis=2)
    place = running_count(present, tok_rows) - 1
    place = jnp.where(present, place, -1)
    spots = jnp.arange(capacity, dtype=jnp.int32)
    picked = place[:, None, :] == spots[None, :, None]
    dispatch = picked.astype(jnp.bfloat16)
    slot_prob = jnp.sum(jnp.where(picked, weight[:, None, :], 0.0), axis=2)

    rows = jnp.einsum(
        "ect,td->ecd", dispatch, hidden_all, preferred_element_type=jnp.float32
    ).astype(jnp.bfloat16)
    gate_act = jnp.einsum("ecd,efd->ecf", rows, gate_w, preferred_element_type=jnp.float32)
    lifted = jnp.einsum("ecd,efd->ecf", rows, up_w, preferred_element_type=jnp.float32)

    def layer_pass(upstream_all):
        up_rows = jnp.einsum(
            "ect,td->ecd", dispatch, upstream_all, preferred_element_type=jnp.float32
        )
        weighted = (slot_prob[:, :, None] * up_rows).astype(jnp.bfloat16)
        back = jnp.einsum("ecd,efd->ecf", weighted, down_w, preferred_element_type=jnp.float32)
        logistic = jax.nn.sigmoid(gate_act)
        d_gate = (back * lifted * logistic * (1.0 + gate_act * (1.0 - logistic))).astype(
            jnp.bfloat16
        )
        d_up = (back * gate_act * logistic).astype(jnp.bfloat16)
        slot_grad = jnp.einsum("ecf,efd->ecd", d_gate, gate_w, preferred_element_type=jnp.float32)
        slot_grad = slot_grad + jnp.einsum(
            "ecf,efd->ecd", d_up, up_w, preferred_element_type=jnp.float32
        )
        partial = jnp.einsum(
            "ect,ecd->td",
            dispatch,
            slot_grad.astype(jnp.bfloat16),
            preferred_element_type=jnp.float32,
        ).astype(jnp.bfloat16)
        return (partial, d_gate, d_up)

    def idle(upstream_all):
        empty = jnp.zeros((local_experts, capacity, units), jnp.bfloat16)
        return (jnp.zeros((tokens, feature_width), jnp.bfloat16), empty, empty)

    partial, gate_upper, up_upper = lax.cond(section_index == 1, layer_pass, idle, cot_all)
    token_grad = reduce_halves(partial, 1, section_index)
    top_inputs = jnp.where(section_index == 1, layer_inputs[0], upper_inputs)
    top_gain = jnp.where(section_index == 1, gain_vector, upper_gain)
    top_normed, top_factor, _ = normalize(top_inputs, top_gain)
    upper_grad = finish(token_grad, top_gain, top_normed, top_factor, cotangent)

    upper_all = gather_halves(upper_grad, 0, section_index)
    partial, gate_lower, up_lower = lax.cond(section_index == 0, layer_pass, idle, upper_all)
    token_grad = reduce_halves(partial, 0, section_index)
    lower_grad = finish(token_grad, gain_vector, normed, factor, upper_grad)
    result = jnp.where(section_index == 1, upper_grad, lower_grad)

    def weigh_rows(operands):
        gate_in, up_in, rows_in = operands
        return (
            jnp.einsum("ecf,ecd->efd", gate_in, rows_in, preferred_element_type=jnp.float32),
            jnp.einsum("ecf,ecd->efd", up_in, rows_in, preferred_element_type=jnp.float32),
        )

    def zero_rows(operands):
        empty = jnp.zeros((local_experts, units, feature_width), jnp.float32)
        return (empty, empty)

    d_gate = jnp.where(section_index == 1, gate_upper, gate_lower)
    d_up = jnp.where(section_index == 1, up_upper, up_lower)
    gate_share, up_share = lax.cond(training, weigh_rows, zero_rows, (d_gate, d_up, rows))
    return (result[None], gate_share[None], up_share[None])


def solution(mesh):
    placed = (
        P("section", OWNERS, None),
        P("section", None),
        P("section", "expert", "mp", None),
        P("section", "expert", "mp", None),
        P("section", "expert", "mp", None),
        P("section", OWNERS, None),
        P("section", OWNERS, None),
        P(OWNERS, None),
        P(),
    )
    return jax.shard_map(
        per_device,
        mesh=mesh,
        in_specs=placed,
        out_specs=(
            P("section", OWNERS, None),
            P("section", "expert", "mp", None),
            P("section", "expert", "mp", None),
        ),
        check_vma=False,
    )
```

time: 2150 us -> 623 us (0.29)
  the two profiles are of different devices: /device:TPU:0 before, /device:TPU:1 now
where the time goes in v1:
time: 623 us; the launch traced here: 618 us
  waiting for transfers between devices  344 us (55%)
  matrix products  134 us (22%)
  blocking collectives  35.7 us (6%)
  starting transfers between devices  30.9 us (5%)
  other arithmetic  25.1 us (4%)
  local copies, waits for them, and re-layouts  24.4 us (4%)
  between operations  15 us (2%)
  loops' own time  9.16 us (1%)
    reduce_scatter x2, waiting for transfers between devices, reduce_halves(): total = lax.psum_scatter(mine, OWNERS, scatter_dimension=0, tiled=True)  137 us
    all_gather x2, waiting for transfers between devices, gather_halves(): lax.all_gather(half_of(rows, section_index), OWNERS, axis=0, tiled=True)  81.2 us
    all_gather x1, waiting for transfers between devices, per_device(): hidden_all = lax.all_gather(hidden, OWNERS, axis=0, tiled=True)  64.5 us
    ppermute x2, waiting for transfers between devices, reduce_halves(): other = lax.ppermute(away, 'section', [(source, 1 - source)])  55.2 us
    all_gather x1, blocking collectives, per_device(): meta = lax.all_gather(meta, OWNERS, axis=0, tiled=True)  35.7 us
    dot_general x1, matrix products, layer_pass(): jnp.einsum('ecd,efd->ecf', weighted, down_w, preferred_element_type=jnp.f...  24.4 us
    ppermute x4, starting transfers between devices, swapped(): return lax.ppermute(x, 'section', [(0, 1), (1, 0)])  23.2 us
    dot_general x1, matrix products, layer_pass(): jnp.einsum('ect,ecd->td', dispatch, slot_grad.astype(jnp.bfloat16), prefe...  21.1 us
  transfers between devices with their start and end apart: 13, of which 11 were waited for; matrix products, arithmetic and copies ran while one was open for 8% of the time, Pallas kernels for 0%

profile of v1, /device:TPU:1, one launch (start us, length us, event | category | flops | bytes accessed | tf_op | source)
XLA Modules:
  0.0 617.9 jit_solution(2785576161719669402)
XLA Ops:
  10.7 1.9 fusion.39
  14.1 35.7 %all-gather = f32[16,64,16]{1,2,0:T(8,128)S(1)} all-gather(f32[1,64,16]{1,2,0:T(8,128)S(1)} %maximum_bitcast_fusion), channel_id=1, replica_groups=mesh['section'=2,'expert'=4,'mp'=4] {'expert','mp'}, dimensions={0}, use_global_device_ids=true | all-gather | bytes 69632 | tf_op jit(solution)/shard_map/all_gather | solution.py:85
  50.0 24.0 %all-gather.5.cloned.1.call-done = bf16[1024,1024]{1,0:T(8,128)(2,1)} async-done(((bf16[64,1024]{1,0:T(8,128)(2,1)}), bf16[1024,1024]{1,0:T(8,128)(2,1)}) %all-gather.5.cloned.1.call-update) | async-done | bytes 2097168 | tf_op jit(solution)/shard_map/all_gather | solution.py:37
  76.7 4.4 fusion.25
  84.4 2.5 pad_maximum_fusion
  86.9 64.5 %all-gather.7.cloned.1.call-done = bf16[1024,2048]{1,0:T(8,128)(2,1)} async-done(((bf16[64,2048]{1,0:T(8,128)(2,1)}), bf16[1024,2048]{1,0:T(8,128)(2,1)}) %all-gather.7.cloned.1.call-update) | async-done | bytes 4194320 | tf_op jit(solution)/shard_map/all_gather | solution.py:88
  151.3 13.9 %fusion.26 = bf16[16,160,2048]{2,1,0:T(8,128)(2,1)S(1)} fusion(s32[16,1024]{1,0:T(8,128)S(1)} %broadcast_select_fusion.9, bf16[1024,2048]{1,0:T(8,128)(2,1)} %all-gather.7.cloned.1.call-done), kind=kOutput, calls=%fused_computation.36 | convolution fusion | flops 10745282560 | bytes 14745600 | tf_op jit(solution)/shard_map/ect,td->ecd/dot_general | solution.py:102
  165.2 14.3 %fusion.63 = f32[16,160,192]{2,1,0:T(8,128)} fusion(bf16[16,160,2048]{2,1,0:T(8,128)(2,1)S(1)} %fusion.26, bf16[1,16,192,2048]{3,2,1,0:T(8,128)(2,1)} %param.17), kind=kOutput, calls=%fused_computation.111 | convolution fusion | flops 2013265920 | bytes 25034752 | tf_op jit(solution)/shard_map/ecd,efd->ecf/dot_general | solution.py:105
  179.6 10.5 %fusion.65 = f32[16,160,192]{2,1,0:T(8,128)} fusion(bf16[16,160,2048]{2,1,0:T(8,128)(2,1)S(1)} %fusion.26, bf16[1,16,192,2048]{3,2,1,0:T(8,128)(2,1)} %param.18), kind=kOutput, calls=%fused_computation.113 | convolution fusion | flops 2013265920 | bytes 25034752 | tf_op jit(solution)/shard_map/ecd,efd->ecf/dot_general | solution.py:106
  190.1 61.3 %conditional.3 = (bf16[1024,2048]{0,1:T(8,128)(2,1)}, bf16[16,160,192]{2,1,0:T(8,128)(2,1)}, bf16[16,160,192]{2,1,0:T(8,128)(2,1)}) conditional(s32[]{:T(128)} %convert_element_type.102, () %tuple.39, (f32[16,160]{1,0:T(8,128)S(1)}, bf16[16,160,1024]{2,1,0:T(8,128)(2,1)}, bf16[1024,2048]{1,0:T(8,128)(2,1)}, bf16[16,192,2048]{2,1,0:T(8,128)(2,1)}, ...), branch_computations={%region_5.6_spmd, %region_6.7_spmd} | conditional | flops 27544092672 | bytes 106440728 | solution.py:135
  190.1 24.4 %multiply_convert_fusion.2 = (bf16[16,160,192]{2,1,0:T(8,128)(2,1)}, bf16[16,160,192]{2,1,0:T(8,128)(2,1)}) fusion(f32[16,160,192]{2,1,0:T(8,128)} %get-tuple-element.67, f32[16,160,192]{2,1,0:T(8,128)} %get-tuple-element.66, bf16[16,192,2048]{2,1,0:T(8,128)(2,1)} %get-tuple-element.65, f32[16,160]{1,0:T(8,128)S(1)} %get-tuple-element.62, ...), kind=kOutput, calls=%fused_computation.10 | convolution fusion | flops 12767559680 | bytes 27928576 | tf_op jit(solution)/shard_map/cond/branch_1_fun/ecd,efd->ecf/dot_general | solution.py:113
  214.5 15.4 %fusion.75 = f32[16,160,2048]{2,1,0:T(8,128)} fusion(bf16[16,160,192]{2,1,0:T(8,128)(2,1)} %get-tuple-element.124, bf16[16,192,2048]{2,1,0:T(8,128)(2,1)} %get-tuple-element.68), kind=kOutput, calls=%fused_computation.119 | convolution fusion | flops 2013265920 | bytes 34537472 | tf_op jit(solution)/shard_map/cond/branch_1_fun/ecf,efd->ecd/dot_general | solution.py:119
  229.9 21.1 %fusion.9 = bf16[1024,2048]{0,1:T(8,128)(2,1)} fusion(bf16[16,160,1024]{2,1,0:T(8,128)(2,1)} %get-tuple-element.63, f32[16,160,2048]{2,1,0:T(8,128)} %fusion.75, bf16[16,160,192]{2,1,0:T(8,128)(2,1)} %get-tuple-element.125, bf16[16,192,2048]{2,1,0:T(8,128)(2,1)} %get-tuple-element.69), kind=kOutput, calls=%fused_computation.9 | convolution fusion | flops 12763267072 | bytes 43974656 | tf_op jit(solution)/shard_map/cond/branch_1_fun/ect,ecd->td/dot_general | solution.py:123
  251.4 6.4 %copy.31 = bf16[1024,2048]{1,0:T(8,128)(2,1)} copy(bf16[1024,2048]{0,1:T(8,128)(2,1)} %get-tuple-element.95) | data formatting | bytes 8388608 | tf_op jit(solution)/shard_map/cond | solution.py:135
  257.8 1.9 slice.33
  261.3 3.6 collective-permute-done.2
  267.9 68.8 %reduce-scatter.3.cloned.1.call-done = bf16[64,1024]{1,0:T(8,128)(2,1)} async-done(((bf16[1024,1024]{1,0:T(8,128)(2,1)}), bf16[64,1024]{1,0:T(8,128)(2,1)}) %reduce-scatter.3.cloned.1.call-update) | async-done | bytes 131088 | tf_op jit(solution)/shard_map/reduce_scatter | solution.py:49
  336.6 11.0 %collective-permute-start.3 = (bf16[64,1024]{1,0:T(8,128)(2,1)}, bf16[64,1024]{1,0:T(8,128)(2,1)S(1)}, u32[]{:S(2)}, u32[]{:S(2)}) collective-permute-start(bf16[64,1024]{1,0:T(8,128)(2,1)} %reduce-scatter.3.cloned.1.call-done), channel_id=1, source_target_pairs={{0,16},{16,0},{1,17},{17,1},{2,18},{18,2},{3,19},{19,3},{4,20},{20... | collective-permute-start | bytes 393224 | tf_op jit(solution)/shard_map/ppermute | solution.py:27
  351.0 57.2 %all-gather.9.cloned.1.call-done = bf16[1024,1024]{1,0:T(8,128)(2,1)} async-done(((bf16[64,1024]{1,0:T(8,128)(2,1)}), bf16[1024,1024]{1,0:T(8,128)(2,1)}) %all-gather.9.cloned.1.call-update) | async-done | bytes 2097168 | tf_op jit(solution)/shard_map/all_gather | solution.py:37
  408.2 3.2 collective-permute-start.5
  411.4 3.8 collective-permute-done.5
  417.1 2.5 pad_maximum_fusion.1
  419.6 13.7 %conditional.4 = (bf16[1024,2048]{0,1:T(8,128)(2,1)}, bf16[16,160,192]{2,1,0:T(8,128)(2,1)}, bf16[16,160,192]{2,1,0:T(8,128)(2,1)}) conditional(s32[]{:T(128)} %convert_element_type.115, () %tuple.41, (f32[16,160]{1,0:T(8,128)S(1)}, bf16[16,160,1024]{2,1,0:T(8,128)(2,1)}, bf16[1024,2048]{1,0:T(8,128)(2,1)}, bf16[16,192,2048]{2,1,0:T(8,128)(2,1)}, ...), branch_computations={%region_9.10_spmd, %region_10.11_spmd} | conditional | flops 27544092672 | bytes 106440728 | solution.py:143
  422.0 2.5 broadcast.82
  433.3 6.4 %copy.33 = bf16[1024,2048]{1,0:T(8,128)(2,1)} copy(bf16[1024,2048]{0,1:T(8,128)(2,1)} %get-tuple-element.96) | data formatting | bytes 8388608 | tf_op jit(solution)/shard_map/cond | solution.py:143
  439.7 1.9 slice.35
  442.9 51.5 %collective-permute-done.6 = bf16[1024,1024]{1,0:T(8,128)(2,1)S(1)} collective-permute-done((bf16[1024,1024]{1,0:T(8,128)(2,1)S(1)}, bf16[1024,1024]{1,0:T(8,128)(2,1)S(1)}, u32[]{:S(2)}, u32[]{:S(2)}) %collective-permute-start.6) | collective-permute-done | bytes 2097184 | tf_op jit(solution)/shard_map/ppermute | solution.py:47
  496.0 67.8 %reduce-scatter.5.cloned.1.call-done = bf16[64,1024]{1,0:T(8,128)(2,1)} async-done(((bf16[1024,1024]{1,0:T(8,128)(2,1)}), bf16[64,1024]{1,0:T(8,128)(2,1)}) %reduce-scatter.5.cloned.1.call-update) | async-done | bytes 131088 | tf_op jit(solution)/shard_map/reduce_scatter | solution.py:49
  563.8 11.6 %collective-permute-start.7 = (bf16[64,1024]{1,0:T(8,128)(2,1)}, bf16[64,1024]{1,0:T(8,128)(2,1)S(1)}, u32[]{:S(2)}, u32[]{:S(2)}) collective-permute-start(bf16[64,1024]{1,0:T(8,128)(2,1)} %reduce-scatter.5.cloned.1.call-done), channel_id=1, source_target_pairs={{0,16},{16,0},{1,17},{17,1},{2,18},{18,2},{3,19},{19,3},{4,20},{20... | collective-permute-start | bytes 393224 | tf_op jit(solution)/shard_map/ppermute | solution.py:27
  576.2 33.7 %conditional.5 = (f32[1,16,192,2048]{3,2,1,0:T(8,128)}, f32[1,16,192,2048]{3,2,1,0:T(8,128)}) conditional(s32[]{:T(128)} %convert_element_type.118, () %tuple.43, (pred[]{:T(512)}, bf16[16,160,192]{2,1,0:T(8,128)(2,1)}, bf16[16,160,192]{2,1,0:T(8,128)(2,1)}, bf16[16,160,2048]{2,1,0:T(8,128)(2,1)}, bf16[16,160,192]{2,1,0:T(8,128)(2,1)}, ...), branch_computations={%region_13.14_spmd, %region_14.15_spmd} | conditional | flops 4027514880 | bytes 75235344 | solution.py:161
  576.2 16.8 %convolution_bitcast_fusion.1 = f32[1,16,192,2048]{3,2,1,0:T(8,128)} fusion(bf16[16,160,2048]{2,1,0:T(8,128)(2,1)} %get-tuple-element.81, bf16[16,160,192]{2,1,0:T(8,128)(2,1)} %get-tuple-element.79, bf16[16,160,192]{2,1,0:T(8,128)(2,1)} %get-tuple-element.80, pred[]{:T(512)} %get-tuple-element.78), kind=kOutput, calls=%fused_computation.27 | convolution fusion | flops 2013757440 | bytes 37617664 | tf_op jit(solution)/shard_map/cond/branch_1_fun/ecf,ecd->efd/dot_general | solution.py:151
  593.0 16.8 %convolution_bitcast_fusion = f32[1,16,192,2048]{3,2,1,0:T(8,128)} fusion(bf16[16,160,2048]{2,1,0:T(8,128)(2,1)} %get-tuple-element.81, bf16[16,160,192]{2,1,0:T(8,128)(2,1)} %get-tuple-element.82, bf16[16,160,192]{2,1,0:T(8,128)(2,1)} %get-tuple-element.83, pred[]{:T(512)} %get-tuple-element.78), kind=kOutput, calls=%fused_computation.26 | convolution fusion | flops 2013757440 | bytes 37617664 | tf_op jit(solution)/shard_map/cond/branch_1_fun/ecf,ecd->efd/dot_general | solution.py:152
  (77 shorter events, 27.1 us)
Async XLA Ops:
  7.2 66.8 %all-gather.5.cloned.1.call-start = ((), (), s32[]{:S(2)}) async-start(), calls=%async_computation.2 | async-start | bytes 2228224 | tf_op jit(solution)/shard_map/all_gather | solution.py:37
  8.8 142.5 %all-gather.7.cloned.1.call-start = ((), (), s32[]{:S(2)}) async-start(), calls=%async_computation.3 | async-start | bytes 4456448 | tf_op jit(solution)/shard_map/all_gather | solution.py:88
  8.9 1.8 collective-permute-start
  10.1 2.5 copy-start.8
  12.6 324.0 %reduce-scatter.3.cloned.1.call-start = ((), (), s32[]{:S(2)}) async-start(), calls=%async_computation.4 | async-start | bytes 2228224 | tf_op jit(solution)/shard_map/reduce_scatter | solution.py:49
  73.9 8.5 %copy-start.4 = (bf16[1024,1024]{1,0:T(8,128)(2,1)S(1)}, bf16[1024,1024]{1,0:T(8,128)(2,1)}, u32[]{:S(2)}) copy-start(bf16[1024,1024]{1,0:T(8,128)(2,1)} %all-gather.5.cloned.1.call-done) | copy-start | bytes 6291460
  73.9 8.5 %collective-permute-start.1 = (bf16[1024,1024]{1,0:T(8,128)(2,1)}, bf16[1024,1024]{1,0:T(8,128)(2,1)}, u32[]{:S(2)}, u32[]{:S(2)}) collective-permute-start(bf16[1024,1024]{1,0:T(8,128)(2,1)} %all-gather.5.cloned.1.call-done), channel_id=1, source_target_pairs={{0,16},{1,17},{2,18},{3,19},{4,20},{5,21},{6,22},{7,23},{8,24},{9,... | collective-permute-start | bytes 6291464 | tf_op jit(solution)/shard_map/ppermute | solution.py:38
  165.2 14.4 %copy-start = (bf16[16,160,2048]{2,1,0:T(8,128)(2,1)}, bf16[16,160,2048]{2,1,0:T(8,128)(2,1)S(1)}, u32[]{:S(2)}) copy-start(bf16[16,160,2048]{2,1,0:T(8,128)(2,1)S(1)} %fusion.26) | copy-start | bytes 31457284
  257.8 7.1 %copy-start.1 = (bf16[1024,2048]{1,0:T(8,128)(2,1)S(1)}, bf16[1024,2048]{1,0:T(8,128)(2,1)}, u32[]{:S(2)}) copy-start(bf16[1024,2048]{1,0:T(8,128)(2,1)} %copy.31) | copy-start | bytes 12582916
  259.7 6.8 %copy-start.6 = (f32[1,2048]{1,0:T(1,128)S(1)}, f32[1,2048]{1,0:T(1,128)}, u32[]{:S(2)}) copy-start(f32[1,2048]{1,0:T(1,128)} %param.16) | copy-start | bytes 24580
  259.8 90.3 %copy-start.5 = (bf16[64,2048]{1,0:T(8,128)(2,1)S(1)}, bf16[64,2048]{1,0:T(8,128)(2,1)}, u32[]{:S(2)}) copy-start(bf16[64,2048]{1,0:T(8,128)(2,1)} %param.22) | copy-start | bytes 786436
  259.8 5.2 collective-permute-start.2
  266.5 141.7 %all-gather.9.cloned.1.call-start = ((), (), s32[]{:S(2)}) async-start(), calls=%async_computation.5 | async-start | bytes 2228224 | tf_op jit(solution)/shard_map/all_gather | solution.py:37
  266.6 1.3 collective-permute-start.4
  336.6 12.2 %collective-permute-start.3 = (bf16[64,1024]{1,0:T(8,128)(2,1)}, bf16[64,1024]{1,0:T(8,128)(2,1)S(1)}, u32[]{:S(2)}, u32[]{:S(2)}) collective-permute-start(bf16[64,1024]{1,0:T(8,128)(2,1)} %reduce-scatter.3.cloned.1.call-done), channel_id=1, source_target_pairs={{0,16},{16,0},{1,17},{17,1},{2,18},{18,2},{3,19},{19,3},{4,20},{20... | collective-permute-start | bytes 393224 | tf_op jit(solution)/shard_map/ppermute | solution.py:27
  351.0 212.9 %reduce-scatter.5.cloned.1.call-start = ((), (), s32[]{:S(2)}) async-start(), calls=%async_computation.6 | async-start | bytes 2228224 | tf_op jit(solution)/shard_map/reduce_scatter | solution.py:49
  408.2 7.0 %collective-permute-start.5 = (bf16[1024,1024]{1,0:T(8,128)(2,1)}, bf16[1024,1024]{1,0:T(8,128)(2,1)S(1)}, u32[]{:S(2)}, u32[]{:S(2)}) collective-permute-start(bf16[1024,1024]{1,0:T(8,128)(2,1)} %all-gather.9.cloned.1.call-done), channel_id=1, source_target_pairs={{16,0},{17,1},{18,2},{19,3},{20,4},{21,5},{22,6},{23,7},{24,8},{25... | collective-permute-start | bytes 6291464 | tf_op jit(solution)/shard_map/ppermute | solution.py:38
  439.7 54.8 %copy-start.2 = (bf16[1024,2048]{1,0:T(8,128)(2,1)S(1)}, bf16[1024,2048]{1,0:T(8,128)(2,1)}, u32[]{:S(2)}) copy-start(bf16[1024,2048]{1,0:T(8,128)(2,1)} %copy.33) | copy-start | bytes 12582916
  441.6 52.8 %collective-permute-start.6 = (bf16[1024,1024]{1,0:T(8,128)(2,1)S(1)}, bf16[1024,1024]{1,0:T(8,128)(2,1)S(1)}, u32[]{:S(2)}, u32[]{:S(2)}) collective-permute-start(bf16[1024,1024]{1,0:T(8,128)(2,1)S(1)} %slice.35), channel_id=1, source_target_pairs={{0,16},{1,17},{2,18},{3,19},{4,20},{5,21},{6,22},{7,23},{8,24},{9,... | collective-permute-start | bytes 6291464 | tf_op jit(solution)/shard_map/ppermute | solution.py:47
  563.8 46.0 %collective-permute-start.7 = (bf16[64,1024]{1,0:T(8,128)(2,1)}, bf16[64,1024]{1,0:T(8,128)(2,1)S(1)}, u32[]{:S(2)}, u32[]{:S(2)}) collective-permute-start(bf16[64,1024]{1,0:T(8,128)(2,1)} %reduce-scatter.5.cloned.1.call-done), channel_id=1, source_target_pairs={{0,16},{16,0},{1,17},{17,1},{2,18},{18,2},{3,19},{19,3},{4,20},{20... | collective-permute-start | bytes 393224 | tf_op jit(solution)/shard_map/ppermute | solution.py:27
  576.1 33.7 %copy-start.7 = (bf16[64,1024]{1,0:T(8,128)(2,1)S(1)}, bf16[64,1024]{1,0:T(8,128)(2,1)}, u32[]{:S(2)}) copy-start(bf16[64,1024]{1,0:T(8,128)(2,1)} %reduce-scatter.5.cloned.1.call-done) | copy-start | bytes 393220
  576.1 33.8 %copy-start.3 = (bf16[1,64,2048]{2,1,0:T(8,128)(2,1)S(1)}, bf16[1,64,2048]{2,1,0:T(8,128)(2,1)}, u32[]{:S(2)}) copy-start(bf16[1,64,2048]{2,1,0:T(8,128)(2,1)} %param.15) | copy-start | bytes 786436
  576.2 33.8 %copy-start.9 = (f32[64]{0:T(128)S(1)}, f32[64]{0:T(128)}, u32[]{:S(2)}) copy-start(f32[64]{0:T(128)} %copy-done.8) | copy-start | bytes 772
Sparse Core Ops, SparseCore 0:
  11.3 62.5 all-gather.4
  77.3 73.9 all-gather.6
  266.7 69.9 reduce-scatter.2
  351.1 57.0 all-gather.8
  496.2 67.6 reduce-scatter.4

commit v2 on v1

--- a/solution.py
+++ b/solution.py
@@ -9,6 +9,21 @@
 epsilon = 1e-06
 
 OWNERS = ("expert", "mp")
+
+
+def pack_meta(own_routes, own_probs):
+    high = lax.reduce_precision(own_probs, 8, 7)
+    middle = lax.reduce_precision(own_probs - high, 8, 7)
+    low = own_probs - high - middle
+    digits = [(own_routes // 128).astype(jnp.float32), (own_routes % 128).astype(jnp.float32)]
+    packed = jnp.concatenate(digits + [high, middle, low], axis=1).astype(jnp.bfloat16)
+    return jnp.pad(packed, ((0, 0), (0, -packed.shape[1] % 128)))
+
+
+def unpack_meta(packed, count):
+    values = packed[:, : 5 * count].astype(jnp.float32)
+    parts = [values[:, i * count : (i + 1) * count] for i in range(5)]
+    return ((parts[0] * 128.0 + parts[1]).astype(jnp.int32), parts[2] + parts[3] + parts[4])
 
 
 def normalize(inputs, gain_vector):
@@ -46,7 +61,10 @@
         away, kept = (kept, away)
     other = lax.ppermute(away, "section", [(source, 1 - source)])
     mine = jnp.where(section_index == source, kept, other)
-    total = lax.psum_scatter(mine, OWNERS, scatter_dimension=0, tiled=True)
+    return lax.psum_scatter(mine, OWNERS, scatter_dimension=0, tiled=True)
+
+
+def whole_rows(total, section_index):
     return joined(total, swapped(total), section_index).astype(jnp.float32)
 
 
@@ -81,12 +99,11 @@
     upper_inputs = swapped(layer_inputs[0])
     upper_gain = swapped(norm_gain[0])
 
-    meta = jnp.concatenate([routes[0].astype(jnp.float32), probs[0]], axis=1)
-    meta = lax.all_gather(meta, OWNERS, axis=0, tiled=True)
-    all_routes = meta[:, :top_count].astype(jnp.int32)
-    all_probs = meta[:, top_count:]
-    hidden_all = lax.all_gather(hidden, OWNERS, axis=0, tiled=True)
-    cot_all = gather_halves(cotangent, 1, section_index)
+    sent = jnp.concatenate([hidden, pack_meta(routes[0], probs[0])], axis=1)
+    sent_all = lax.all_gather(sent, OWNERS, axis=0, tiled=True)
+    hidden_all = sent_all[:, :feature_width]
+    all_routes, all_probs = unpack_meta(sent_all[:, feature_width:], top_count)
+    cot_half = lax.all_gather(half_of(cotangent, section_index), OWNERS, axis=0, tiled=True)
 
     own = lax.axis_index("expert") * local_experts + jnp.arange(local_experts, dtype=jnp.int32)
     match = all_routes[None, :, :] == own[:, None, None]
@@ -105,6 +122,10 @@
     gate_act = jnp.einsum("ecd,efd->ecf", rows, gate_w, preferred_element_type=jnp.float32)
     lifted = jnp.einsum("ecd,efd->ecf", rows, up_w, preferred_element_type=jnp.float32)
 
+    cot_half, rows, gate_act, lifted = lax.optimization_barrier((cot_half, rows, gate_act, lifted))
+    cot_other = lax.ppermute(cot_half, "section", [(0, 1)])
+    cot_all = joined(cot_half, cot_other, section_index)
+
     def layer_pass(upstream_all):
         up_rows = jnp.einsum(
             "ect,td->ecd", dispatch, upstream_all, preferred_element_type=jnp.float32
@@ -133,7 +154,7 @@
         return (jnp.zeros((tokens, feature_width), jnp.bfloat16), empty, empty)
 
     partial, gate_upper, up_upper = lax.cond(section_index == 1, layer_pass, idle, cot_all)
-    token_grad = reduce_halves(partial, 1, section_index)
+    token_grad = whole_rows(reduce_halves(partial, 1, section_index), section_index)
     top_inputs = jnp.where(section_index == 1, layer_inputs[0], upper_inputs)
     top_gain = jnp.where(section_index == 1, gain_vector, upper_gain)
     top_normed, top_factor, _ = normalize(top_inputs, top_gain)
@@ -141,9 +162,7 @@
 
     upper_all = gather_halves(upper_grad, 0, section_index)
     partial, gate_lower, up_lower = lax.cond(section_index == 0, layer_pass, idle, upper_all)
-    token_grad = reduce_halves(partial, 0, section_index)
-    lower_grad = finish(token_grad, gain_vector, normed, factor, upper_grad)
-    result = jnp.where(section_index == 1, upper_grad, lower_grad)
+    total = reduce_halves(partial, 0, section_index)
 
     def weigh_rows(operands):
         gate_in, up_in, rows_in = operands
@@ -159,6 +178,10 @@
     d_gate = jnp.where(section_index == 1, gate_upper, gate_lower)
     d_up = jnp.where(section_index == 1, up_upper, up_lower)
     gate_share, up_share = lax.cond(training, weigh_rows, zero_rows, (d_gate, d_up, rows))
+    total, gate_share, up_share = lax.optimization_barrier((total, gate_share, up_share))
+    token_grad = whole_rows(total, section_index)
+    lower_grad = finish(token_grad, gain_vector, normed, factor, upper_grad)
+    result = jnp.where(section_index == 1, upper_grad, lower_grad)
     return (result[None], gate_share[None], up_share[None])
 
 

time: 623 us -> 578 us (0.928)
  the two profiles are of different devices: /device:TPU:1 before, /device:TPU:0 now
where the time goes in v2:
time: 578 us; the launch traced here: 570 us
  waiting for transfers between devices  361 us (62%)
  matrix products  99.8 us (17%)
  local copies, waits for them, and re-layouts  47 us (8%)
  other arithmetic  27.6 us (5%)
  starting transfers between devices  18.6 us (3%)
  between operations  15.1 us (3%)
    all_gather x1, waiting for transfers between devices, per_device(): sent_all = lax.all_gather(sent, OWNERS, axis=0, tiled=True)  78.9 us
    reduce_scatter x1, waiting for transfers between devices, reduce_halves(): return lax.psum_scatter(mine, OWNERS, scatter_dimension=0, tiled=True)  77.9 us
    ppermute x2, waiting for transfers between devices, reduce_halves(): other = lax.ppermute(away, 'section', [(source, 1 - source)])  61.2 us
    all_gather x1, waiting for transfers between devices, gather_halves(): lax.all_gather(half_of(rows, section_index), OWNERS, axis=0, tiled=True)  58 us
    unnamed x6, waiting for transfers between devices  54.6 us
    another operation x5, local copies, waits for them, and re-layouts  29.3 us
    dot_general x1, matrix products, layer_pass(): jnp.einsum('ecd,efd->ecf', weighted, down_w, preferred_element_type=jnp.f...  24.3 us
    all_gather x1, waiting for transfers between devices, per_device(): lax.all_gather(half_of(cotangent, section_index), OWNERS, axis=0, tiled=T...  21.8 us
  transfers between devices with their start and end apart: 13, of which 11 were waited for; matrix products, arithmetic and copies ran while one was open for 14% of the time, Pallas kernels for 0%

profile of v2, /device:TPU:0, one launch (start us, length us, event | category | flops | bytes accessed | tf_op | source)
XLA Modules:
  0.0 569.7 jit_solution(1012010558492975969)
XLA Ops:
  16.2 78.9 %all-gather.4.cloned.1.call-done = bf16[1024,2176]{1,0:T(8,128)(2,1)} async-done(((bf16[64,2176]{1,0:T(8,128)(2,1)}), bf16[1024,2176]{1,0:T(8,128)(2,1)}) %all-gather.4.cloned.1.call-update) | async-done | bytes 4456464 | tf_op jit(solution)/shard_map/all_gather | solution.py:103
  97.3 13.7 %fusion.28 = bf16[16,160,2048]{2,1,0:T(8,128)(2,1)S(1)} fusion(s32[16,1024]{1,0:T(8,128)S(1)} %broadcast_select_fusion.9, bf16[1024,2176]{1,0:T(8,128)(2,1)} %all-gather.4.cloned.1.call-done), kind=kOutput, calls=%fused_computation.36 | convolution fusion | flops 10745282560 | bytes 14745600 | tf_op jit(solution)/shard_map/ect,td->ecd/dot_general | solution.py:119
  111.1 14.3 %fusion.75 = f32[16,160,192]{2,1,0:T(8,128)} fusion(bf16[16,160,2048]{2,1,0:T(8,128)(2,1)S(1)} %fusion.28, bf16[1,16,192,2048]{3,2,1,0:T(8,128)(2,1)} %param.18), kind=kOutput, calls=%fused_computation.140 | convolution fusion | flops 2013265920 | bytes 25034752 | tf_op jit(solution)/shard_map/ecd,efd->ecf/dot_general | solution.py:123
  125.4 10.6 %fusion.77 = f32[16,160,192]{2,1,0:T(8,128)} fusion(bf16[16,160,2048]{2,1,0:T(8,128)(2,1)S(1)} %fusion.28, bf16[1,16,192,2048]{3,2,1,0:T(8,128)(2,1)} %param.17), kind=kOutput, calls=%fused_computation.142 | convolution fusion | flops 2013265920 | bytes 25034752 | tf_op jit(solution)/shard_map/ecd,efd->ecf/dot_general | solution.py:122
  136.0 21.8 %all-gather.6.cloned.1.call-done = bf16[1024,1024]{1,0:T(8,128)(2,1)} async-done(((bf16[64,1024]{1,0:T(8,128)(2,1)}), bf16[1024,1024]{1,0:T(8,128)(2,1)}) %all-gather.6.cloned.1.call-update) | async-done | bytes 2097168 | tf_op jit(solution)/shard_map/all_gather | solution.py:106
  157.8 3.0 collective-permute-start.1
  161.0 4.4 fusion.27
  166.8 1.9 broadcast_select_fusion.3
  168.6 2.5 pad_maximum_fusion
  171.1 5.0 conditional.3
  173.6 2.5 broadcast.89
  176.1 1.8 slice.48
  177.9 12.0 %collective-permute-start.2 = (bf16[1024,1024]{0,1:T(8,128)(2,1)S(1)}, bf16[1024,1024]{0,1:T(8,128)(2,1)S(1)}, u32[]{:S(2)}, u32[]{:S(2)}) collective-permute-start(bf16[1024,1024]{0,1:T(8,128)(2,1)S(1)} %slice.48), channel_id=1, source_target_pairs={{16,0},{17,1},{18,2},{19,3},{20,4},{21,5},{22,6},{23,7},{24,8},{25... | collective-permute-start | bytes 6291464 | tf_op jit(solution)/shard_map/ppermute | solution.py:62
  189.9 57.5 %collective-permute-done.2 = bf16[1024,1024]{0,1:T(8,128)(2,1)S(1)} collective-permute-done((bf16[1024,1024]{0,1:T(8,128)(2,1)S(1)}, bf16[1024,1024]{0,1:T(8,128)(2,1)S(1)}, u32[]{:S(2)}, u32[]{:S(2)}) %collective-permute-start.2) | collective-permute-done | bytes 2097184 | tf_op jit(solution)/shard_map/ppermute | solution.py:62
  247.4 1.8 slice_select_fusion.1
  249.2 2.6 copy.50
  253.1 77.9 %reduce-scatter.7.cloned.1.call-done = bf16[64,1024]{1,0:T(8,128)(2,1)} async-done(((bf16[1024,1024]{1,0:T(8,128)(2,1)}), bf16[64,1024]{1,0:T(8,128)(2,1)}) %reduce-scatter.7.cloned.1.call-update) | async-done | bytes 131088 | tf_op jit(solution)/shard_map/reduce_scatter | solution.py:64
  334.7 58.0 %all-gather.8.cloned.1.call-done = bf16[1024,1024]{1,0:T(8,128)(2,1)} async-done(((bf16[64,1024]{1,0:T(8,128)(2,1)}), bf16[1024,1024]{1,0:T(8,128)(2,1)}) %all-gather.8.cloned.1.call-update) | async-done | bytes 2097168 | tf_op jit(solution)/shard_map/all_gather | solution.py:52
  394.0 5.0 collective-permute-done.5
  399.0 1.9 broadcast_select_fusion.1
  400.9 2.5 pad_maximum_fusion.1
  403.4 61.0 %conditional.4 = (bf16[1024,2048]{0,1:T(8,128)(2,1)}, bf16[16,160,192]{2,1,0:T(8,128)(2,1)}, bf16[16,160,192]{2,1,0:T(8,128)(2,1)}) conditional(s32[]{:T(128)} %convert_element_type.122, () %tuple.40, (f32[16,160]{1,0:T(8,128)S(1)}, bf16[16,160,1024]{2,1,0:T(8,128)(2,1)}, bf16[1024,2048]{1,0:T(8,128)(2,1)}, bf16[16,192,2048]{2,1,0:T(8,128)(2,1)}, ...), branch_computations={%region_9.10_spmd, %region_10.11_spmd} | conditional | flops 27544092672 | bytes 106440728 | solution.py:164
  403.4 24.3 %multiply_convert_fusion.6 = (bf16[16,160,192]{2,1,0:T(8,128)(2,1)}, bf16[16,160,192]{2,1,0:T(8,128)(2,1)}) fusion(f32[16,160,192]{2,1,0:T(8,128)} %get-tuple-element.73, f32[16,160,192]{2,1,0:T(8,128)} %get-tuple-element.72, bf16[16,192,2048]{2,1,0:T(8,128)(2,1)} %get-tuple-element.71, f32[16,160]{1,0:T(8,128)S(1)} %get-tuple-element.68, ...), kind=kOutput, calls=%fused_computation.23 | convolution fusion | flops 12767559680 | bytes 27928576 | tf_op jit(solution)/shard_map/cond/branch_1_fun/ecd,efd->ecf/dot_general | solution.py:134
  427.7 15.4 %fusion.88 = f32[16,160,2048]{2,1,0:T(8,128)} fusion(bf16[16,160,192]{2,1,0:T(8,128)(2,1)} %get-tuple-element.161, bf16[16,192,2048]{2,1,0:T(8,128)(2,1)} %get-tuple-element.74), kind=kOutput, calls=%fused_computation.149 | convolution fusion | flops 2013265920 | bytes 34537472 | tf_op jit(solution)/shard_map/cond/branch_1_fun/ecf,efd->ecd/dot_general | solution.py:140
  443.1 21.1 %fusion.19 = bf16[1024,2048]{0,1:T(8,128)(2,1)} fusion(bf16[16,160,1024]{2,1,0:T(8,128)(2,1)} %get-tuple-element.69, f32[16,160,2048]{2,1,0:T(8,128)} %fusion.88, bf16[16,160,192]{2,1,0:T(8,128)(2,1)} %get-tuple-element.162, bf16[16,192,2048]{2,1,0:T(8,128)(2,1)} %get-tuple-element.75), kind=kOutput, calls=%fused_computation.22 | convolution fusion | flops 12763267072 | bytes 43974656 | tf_op jit(solution)/shard_map/cond/branch_1_fun/ect,ecd->td/dot_general | solution.py:144
  464.4 6.4 %copy.44 = bf16[1024,2048]{1,0:T(8,128)(2,1)} copy(bf16[1024,2048]{0,1:T(8,128)(2,1)} %get-tuple-element.104) | data formatting | bytes 8388608 | tf_op jit(solution)/shard_map/cond | solution.py:164
  470.8 1.9 slice.60
  474.2 3.6 collective-permute-done.6
  480.1 24.3 %conditional.5 = (f32[16,192,2048]{2,1,0:T(8,128)}, f32[16,192,2048]{2,1,0:T(8,128)}) conditional(s32[]{:T(128)} %convert_element_type.123, () %tuple.42, (pred[]{:T(512)}, bf16[16,160,192]{2,1,0:T(8,128)(2,1)}, bf16[16,160,192]{2,1,0:T(8,128)(2,1)}, bf16[16,160,2048]{2,1,0:T(8,128)(2,1)}, bf16[16,160,192]{2,1,0:T(8,128)(2,1)}, ...), branch_computations={%region_12.13_spmd, %region_13.14_spmd} | conditional | flops 4027514880 | bytes 75235344 | solution.py:180
  480.1 12.1 %broadcast.95.clone = f32[16,192,2048]{2,1,0:T(8,128)} broadcast(f32[]{:T(128)} %constant.66.clone), dimensions={} | broadcast | bytes 25165828 | tf_op jit(solution)/shard_map/broadcast.17
  492.2 12.1 %broadcast.95 = f32[16,192,2048]{2,1,0:T(8,128)} broadcast(f32[]{:T(128)} %constant.66.clone), dimensions={} | broadcast | bytes 25165828 | tf_op jit(solution)/shard_map/broadcast.17
  504.3 54.5 %reduce-scatter.9.cloned.1.call-done = bf16[64,1024]{1,0:T(8,128)(2,1)} async-done(((bf16[1024,1024]{1,0:T(8,128)(2,1)}), bf16[64,1024]{1,0:T(8,128)(2,1)}) %reduce-scatter.9.cloned.1.call-update) | async-done | bytes 131088
  (80 shorter events, 28.3 us)
Async XLA Ops:
  7.2 87.9 %all-gather.4.cloned.1.call-start = ((), (), s32[]{:S(2)}) async-start(), calls=%async_computation.2 | async-start | bytes 4734976 | tf_op jit(solution)/shard_map/all_gather | solution.py:103
  7.2 5.2 collective-permute-start
  12.4 82.6 %copy-start.6 = (f32[64]{0:T(128)}, f32[64]{0:T(128)S(1)}, u32[]{:S(2)}) copy-start(f32[64]{0:T(128)S(1)} %add_rsqrt_fusion) | copy-start | bytes 772
  14.4 143.3 %all-gather.6.cloned.1.call-start = ((), (), s32[]{:S(2)}) async-start(), calls=%async_computation.3 | async-start | bytes 2228224 | tf_op jit(solution)/shard_map/all_gather | solution.py:106
  16.1 315.0 %reduce-scatter.7.cloned.1.call-start = ((), (), s32[]{:S(2)}) async-start(), calls=%async_computation.5 | async-start | bytes 2228224 | tf_op jit(solution)/shard_map/reduce_scatter | solution.py:64
  111.1 14.3 %copy-start = (bf16[16,160,2048]{2,1,0:T(8,128)(2,1)}, bf16[16,160,2048]{2,1,0:T(8,128)(2,1)S(1)}, u32[]{:S(2)}) copy-start(bf16[16,160,2048]{2,1,0:T(8,128)(2,1)S(1)} %fusion.28) | copy-start | bytes 31457284
  157.8 9.0 %copy-start.3 = (bf16[1024,1024]{1,0:T(8,128)(2,1)S(1)}, bf16[1024,1024]{1,0:T(8,128)(2,1)}, u32[]{:S(2)}) copy-start(bf16[1024,1024]{1,0:T(8,128)(2,1)} %all-gather.6.cloned.1.call-done) | copy-start | bytes 6291460
  157.8 9.0 %collective-permute-start.1 = (bf16[1024,1024]{1,0:T(8,128)(2,1)}, bf16[1024,1024]{1,0:T(8,128)(2,1)}, u32[]{:S(2)}, u32[]{:S(2)}) collective-permute-start(bf16[1024,1024]{1,0:T(8,128)(2,1)} %all-gather.6.cloned.1.call-done), channel_id=1, source_target_pairs={{0,16},{1,17},{2,18},{3,19},{4,20},{5,21},{6,22},{7,23},{8,24},{9,... | collective-permute-start | bytes 6291464 | tf_op jit(solution)/shard_map/ppermute | solution.py:126
  177.9 69.5 %collective-permute-start.2 = (bf16[1024,1024]{0,1:T(8,128)(2,1)S(1)}, bf16[1024,1024]{0,1:T(8,128)(2,1)S(1)}, u32[]{:S(2)}, u32[]{:S(2)}) collective-permute-start(bf16[1024,1024]{0,1:T(8,128)(2,1)S(1)} %slice.48), channel_id=1, source_target_pairs={{16,0},{17,1},{18,2},{19,3},{20,4},{21,5},{22,6},{23,7},{24,8},{25... | collective-permute-start | bytes 6291464 | tf_op jit(solution)/shard_map/ppermute | solution.py:62
  249.2 2.7 copy-start.5
  249.2 84.6 %copy-start.4 = (bf16[64,2048]{1,0:T(8,128)(2,1)S(1)}, bf16[64,2048]{1,0:T(8,128)(2,1)}, u32[]{:S(2)}) copy-start(bf16[64,2048]{1,0:T(8,128)(2,1)} %param.22) | copy-start | bytes 786436
  251.8 140.9 %all-gather.8.cloned.1.call-start = ((), (), s32[]{:S(2)}) async-start(), calls=%async_computation.4 | async-start | bytes 2228224 | tf_op jit(solution)/shard_map/all_gather | solution.py:52
  251.9 1.2 collective-permute-start.4
  331.0 1.6 collective-permute-start.3
  334.7 224.2 %reduce-scatter.9.cloned.1.call-start = ((), (), s32[]{:S(2)}) async-start(), calls=%async_computation.6 | async-start | bytes 2228224
  392.8 6.3 %collective-permute-start.5 = (bf16[1024,1024]{1,0:T(8,128)(2,1)}, bf16[1024,1024]{1,0:T(8,128)(2,1)S(1)}, u32[]{:S(2)}, u32[]{:S(2)}) collective-permute-start(bf16[1024,1024]{1,0:T(8,128)(2,1)} %all-gather.8.cloned.1.call-done), channel_id=1, source_target_pairs={{16,0},{17,1},{18,2},{19,3},{20,4},{21,5},{22,6},{23,7},{24,8},{25... | collective-permute-start | bytes 6291464 | tf_op jit(solution)/shard_map/ppermute | solution.py:53
  470.8 7.0 %copy-start.1 = (bf16[1024,2048]{1,0:T(8,128)(2,1)S(1)}, bf16[1024,2048]{1,0:T(8,128)(2,1)}, u32[]{:S(2)}) copy-start(bf16[1024,2048]{1,0:T(8,128)(2,1)} %copy.44) | copy-start | bytes 12582916
  472.8 5.1 collective-permute-start.6
  480.0 81.5 %copy-start.2 = (bf16[1,64,2048]{2,1,0:T(8,128)(2,1)S(1)}, bf16[1,64,2048]{2,1,0:T(8,128)(2,1)}, u32[]{:S(2)}) copy-start(bf16[1,64,2048]{2,1,0:T(8,128)(2,1)} %param.15) | copy-start | bytes 786436
  480.1 81.5 %copy-start.7 = (f32[64]{0:T(128)S(1)}, f32[64]{0:T(128)}, u32[]{:S(2)}) copy-start(f32[64]{0:T(128)} %copy-done.6) | copy-start | bytes 772
  560.1 1.4 collective-permute-start.7
Sparse Core Ops, SparseCore 0:
  14.6 80.4 all-gather.3
  98.4 59.3 all-gather.5
  251.9 79.0 reduce-scatter.6
  334.8 57.8 all-gather.7
  479.5 79.3 reduce-scatter.8
